TPU v7x, 512 devices: a whole 4x4x16 slice. The times are simulated.
512 devices in a mesh: rep: 4 (over y), fsdp: 128 (over z, x, core).
Axes of the slice: x: 4, y: 4, z: 16, core: 2. Of those that a mesh axis runs over, the one named last changes fastest.
Arguments:
- gradient: bfloat16 [4, 64, 512, 512], P('rep', None, 'fsdp'), may hold values from -1.6953125 to 1.6953125
- left_stats: float32 [128, 512, 512], P('fsdp'), as said below
- right_stats: float32 [128, 512, 512], P('fsdp'), as said below
- block_lists: int32 [128, 1], replicated, may hold values from -1 to 63, as said below
- block_counts: int32 [128], replicated, may hold values from 0 to 1, as said below
Outputs:
- direction: bfloat16 [64, 512, 512], P(None, 'fsdp')
- left_new: float32 [128, 512, 512], P('fsdp')
- right_new: float32 [128, 512, 512], P('fsdp')
Inputs may be any that keep to these rules, and one draw needn't show every extreme that they name: `block_lists`: entries k < block_counts[w] of row w name the blocks that worker w preconditions; over all workers each of the 64 blocks is named exactly once; all other entries are -1. block_counts[w] is the number of blocks of worker w; some worker holds exactly 1. `left_stats`: each slot's matrix is symmetric positive definite. `right_stats`: each slot's matrix is symmetric positive definite.
All inputs are finite; a program needn't handle non-finite values. Where the computation divides by a largest or mean magnitude, that divisor is 1e-20 or more.
Results may differ from a plain program's by a relative error of at most 0.015.
Values may be sent and summed in bfloat16 or wider, within the bound.
A program may use at most 64 MiB of HBM per device.

v0:
```python
import jax
import jax.numpy as jnp
from jax import lax
from jax.sharding import PartitionSpec as P

ITERS = 2


decay_rate = 0.95


def hidot(left_mat, right_mat):
    return jnp.dot(
        left_mat, right_mat, precision=lax.Precision.HIGHEST, preferred_element_type=jnp.float32
    )


def inverse_root(matrix):
    dimension = matrix.shape[0]
    identity_mat = jnp.eye(dimension, dtype=jnp.float32)
    row_bound = jnp.max(jnp.sum(jnp.abs(matrix), axis=1))
    factor = 2.5 / row_bound
    current = factor * matrix
    root_est = identity_mat
    for sweep in range(ITERS):
        step_mat = (5.0 * identity_mat - current) * 0.25
        if sweep == 0:
            root_est = jnp.sqrt(jnp.sqrt(factor)) * step_mat
        else:
            root_est = hidot(root_est, step_mat)
        if sweep + 1 < ITERS:
            square = hidot(step_mat, step_mat)
            fourth = hidot(square, square)
            current = hidot(fourth, current)
    return root_est


def precondition(grad_block, left_stat, right_stat):
    gram_left = jnp.dot(grad_block, grad_block.T, preferred_element_type=jnp.float32)
    gram_right = jnp.dot(grad_block.T, grad_block, preferred_element_type=jnp.float32)
    left_next = decay_rate * left_stat + (1.0 - decay_rate) * gram_left
    right_next = decay_rate * right_stat + (1.0 - decay_rate) * gram_right
    left_root = inverse_root(left_next).astype(jnp.bfloat16)
    right_root = inverse_root(right_next).astype(jnp.bfloat16)
    half_step = jnp.dot(left_root, grad_block, preferred_element_type=jnp.float32).astype(
        jnp.bfloat16
    )
    shaped = jnp.dot(half_step, right_root, preferred_element_type=jnp.float32)
    grad_wide = grad_block.astype(jnp.float32)
    grad_norm = jnp.sqrt(jnp.sum(grad_wide * grad_wide))
    shaped_norm = jnp.sqrt(jnp.sum(shaped * shaped) + 1e-06)
    grafted = (shaped * (grad_norm / shaped_norm)).astype(jnp.bfloat16)
    return (grafted, left_next, right_next)


def skip_slot(grad_block, left_stat, right_stat):
    return (jnp.zeros_like(grad_block), left_stat, right_stat)


def local(gradient, left_stats, right_stats, block_lists, block_counts):
    block_total = gradient.shape[1]
    dev_rows = gradient.shape[2]
    block_width = gradient.shape[3]
    workers = lax.axis_size("fsdp")
    slot_count = block_lists.shape[1]
    own_rows = gradient[0].astype(jnp.float32)
    safe_ids = jnp.clip(block_lists, 0, block_total - 1)
    live_table = jnp.arange(slot_count, dtype=jnp.int32)[None, :] < block_counts[:, None]
    targets = jnp.where(live_table, block_lists, block_total).T
    own_live = lax.dynamic_index_in_dim(live_table, lax.axis_index("fsdp"), 0, keepdims=False)
    summed = lax.psum(own_rows.astype(jnp.bfloat16), "rep")
    outgoing = summed[safe_ids.T]
    arrived = lax.all_to_all(outgoing, "fsdp", split_axis=1, concat_axis=1, tiled=True)
    blocks = arrived.reshape(slot_count, workers * dev_rows, block_width)

    def one_slot(slot_items):
        grad_block, left_stat, right_stat, usable = slot_items
        return lax.cond(usable, precondition, skip_slot, grad_block, left_stat, right_stat)

    grafted, left_new, right_new = lax.map(one_slot, (blocks, left_stats, right_stats, own_live))
    returning = lax.all_to_all(
        grafted.reshape(slot_count, workers, dev_rows, block_width),
        "fsdp",
        split_axis=1,
        concat_axis=1,
        tiled=True,
    )
    direction = (
        jnp.zeros((block_total, dev_rows, block_width), jnp.bfloat16)
        .at[targets]
        .set(returning, mode="drop")
    )
    return (direction, left_new, right_new)


def solution(mesh):
    placed = (P("rep", None, "fsdp", None), P("fsdp", None, None), P("fsdp", None, None), P(), P())
    return jax.shard_map(
        local,
        mesh=mesh,
        in_specs=placed,
        out_specs=(P(None, "fsdp", None), P("fsdp", None, None), P("fsdp", None, None)),
        check_vma=False,
    )
```

profile of v0, /device:TPU:1, one launch (start us, length us, event | category | flops | bytes accessed | tf_op | source)
XLA Modules:
  0.0 217.0 jit_solution(13169003189978040345)
XLA Ops:
  7.2 0.0 all-reduce.2.cloned.1.call-start
  7.2 0.0 copy-start.2
  7.2 0.7 all-reduce.2.cloned.1.call-update
  7.9 0.0 copy-done.2
  7.9 0.0 copy-done.3
  7.9 0.0 copy-start.1
  8.0 62.7 %all-reduce.2.cloned.1.call-done = bf16[64,4,512]{2,1,0:T(4,128)(2,1)} async-done(((bf16[64,4,512]{2,1,0:T(4,128)(2,1)}), bf16[64,4,512]{2,1,0:T(4,128)(2,1)}) %all-reduce.2.cloned.1.call-update) | async-done | bytes 262160 | tf_op jit(solution)/shard_map/psum | solution.py:71
  70.6 2.7 %gather_fusion = bf16[128,4,512]{2,1,0:T(4,128)(2,1)} fusion(bf16[64,4,512]{2,1,0:T(4,128)(2,1)} %all-reduce.2.cloned.1.call-done, s32[1024]{0:T(1024)S(1)} %pad_clamp_fusion), kind=kCustom, calls=%fused_computation | custom fusion | bytes 1049088 | tf_op jit(solution)/shard_map/gather | solution.py:72
  73.4 18.7 %all-to-all-start = ((bf16[1,128,4,512]{3,2,0,1:T(4,128)(2,1)}), bf16[1,128,4,512]{3,2,0,1:T(4,128)(2,1)S(1)}, u32[]{:S(2)}, u32[]{:S(2)}) async-start(bf16[1,128,4,512]{3,2,0,1:T(4,128)(2,1)} %bitcast.13), calls=%async_computation | async-start | bytes 1048576 | tf_op jit(solution)/shard_map/all_to_all | solution.py:73
  92.2 0.6 dynamic-slice.3
  93.4 0.3 copy.23
  93.7 1.6 copy.24
  95.3 27.6 %all-to-all-done = bf16[1,128,4,512]{3,2,0,1:T(4,128)(2,1)S(1)} async-done(((bf16[1,128,4,512]{3,2,0,1:T(4,128)(2,1)}), bf16[1,128,4,512]{3,2,0,1:T(4,128)(2,1)S(1)}, u32[]{:S(2)}, u32[]{:S(2)}) %all-to-all-start) | async-done | bytes 524320 | tf_op jit(solution)/shard_map/all_to_all | solution.py:73
  123.0 0.8 conditional.1
  123.0 0.8 broadcast.56
  123.8 2.0 reshape.100
  125.8 48.3 %all-to-all-start.1 = ((bf16[1,128,4,512]{3,2,0,1:T(4,128)(2,1)}), bf16[1,128,4,512]{3,2,0,1:T(4,128)(2,1)S(1)}, u32[]{:S(2)}, u32[]{:S(2)}) async-start(bf16[1,128,4,512]{3,2,0,1:T(4,128)(2,1)} %reshape.100), calls=%async_computation.1 | async-start | bytes 1048576 | tf_op jit(solution)/shard_map/all_to_all | solution.py:81
  174.1 1.3 copy.27
  175.4 1.3 copy.28
  176.7 28.2 %all-to-all-done.1 = bf16[1,128,4,512]{3,2,0,1:T(4,128)(2,1)S(1)} async-done(((bf16[1,128,4,512]{3,2,0,1:T(4,128)(2,1)}), bf16[1,128,4,512]{3,2,0,1:T(4,128)(2,1)S(1)}, u32[]{:S(2)}, u32[]{:S(2)}) %all-to-all-start.1) | async-done | bytes 524320 | tf_op jit(solution)/shard_map/all_to_all | solution.py:81
  204.9 0.1 broadcast_in_dim.23
  205.0 4.5 %scatter_fusion = bf16[64,4,512]{2,1,0:T(4,128)(2,1)S(1)} fusion(bf16[64,4,512]{2,1,0:T(4,128)(2,1)S(1)} %broadcast_in_dim.23, s32[128]{0:T(128)S(1)} %get-tuple-element.59, bf16[128,4,512]{2,1,0:T(4,128)(2,1)S(1)} %bitcast.54), kind=kCustom, calls=%fused_computation.1 | custom fusion | bytes 1573376 | tf_op jit(solution)/shard_map/scatter | solution.py:91
  209.5 0.0 copy-start
  209.5 0.7 copy-done
  (5 shorter events, 0.0 us)
Async XLA Ops:
  7.2 63.5 %all-reduce.2.cloned.1.call-start = ((), (), s32[]{:S(2)}) async-start(), calls=%async_computation.2 | async-start | bytes 524288 | tf_op jit(solution)/shard_map/psum | solution.py:71
  7.2 0.7 copy-start.2
  7.2 0.7 copy-start.3
  7.9 85.5 %copy-start.1 = (f32[1,512,512]{2,1,0:T(8,128)S(1)}, f32[1,512,512]{2,1,0:T(8,128)}, u32[]{:S(2)}) copy-start(f32[1,512,512]{2,1,0:T(8,128)} %param.8) | copy-start | bytes 3145732
  73.4 49.6 %all-to-all-start = ((bf16[1,128,4,512]{3,2,0,1:T(4,128)(2,1)}), bf16[1,128,4,512]{3,2,0,1:T(4,128)(2,1)S(1)}, u32[]{:S(2)}, u32[]{:S(2)}) async-start(bf16[1,128,4,512]{3,2,0,1:T(4,128)(2,1)} %bitcast.13), calls=%async_computation | async-start | bytes 1048576 | tf_op jit(solution)/shard_map/all_to_all | solution.py:73
  125.8 79.2 %all-to-all-start.1 = ((bf16[1,128,4,512]{3,2,0,1:T(4,128)(2,1)}), bf16[1,128,4,512]{3,2,0,1:T(4,128)(2,1)S(1)}, u32[]{:S(2)}, u32[]{:S(2)}) async-start(bf16[1,128,4,512]{3,2,0,1:T(4,128)(2,1)} %reshape.100), calls=%async_computation.1 | async-start | bytes 1048576 | tf_op jit(solution)/shard_map/all_to_all | solution.py:81
  209.5 0.7 copy-start
Sparse Core Ops, SparseCore 0:
  10.3 60.2 all-reduce.1
where the time goes:
time: 219 us; the launch traced here: 217 us
  waiting for transfers between devices  119 us (54%)
  starting transfers between devices  67.1 us (31%)
  local copies, waits for them, and re-layouts  15.9 us (7%)
  between operations  14.8 us (7%)
    psum x1, waiting for transfers between devices, local(): summed = lax.psum(own_rows.astype(jnp.bfloat16), 'rep')  62.7 us
    all_to_all x1, starting transfers between devices, local(): lax.all_to_all(grafted.reshape(slot_count, workers, dev_rows, block_width...  48.3 us
    all_to_all x1, waiting for transfers between devices, local(): lax.all_to_all(grafted.reshape(slot_count, workers, dev_rows, block_width...  28.2 us
    all_to_all x1, waiting for transfers between devices, local(): lax.all_to_all(outgoing, 'fsdp', split_axis=1, concat_axis=1, tiled=True)  27.6 us
    all_to_all x1, starting transfers between devices, local(): lax.all_to_all(outgoing, 'fsdp', split_axis=1, concat_axis=1, tiled=True)  18.7 us
    scatter x1, local copies, waits for them, and re-layouts, local(): direction = jnp.zeros((block_total, dev_rows, block_width), jnp.bfloat16)...  4.47 us
  transfers between devices with their start and end apart: 3, of which 3 were waited for; matrix products, arithmetic and copies ran while one was open for 2% of the time, Pallas kernels for 0%

commit v1 on v0

v1 whole, which is shorter than its diff:
```python
import functools

import jax
import jax.numpy as jnp
from jax import lax
from jax.experimental import pallas as pl
from jax.experimental.pallas import tpu as pltpu
from jax.sharding import PartitionSpec as P

DECAY = 0.95
LANES = 8
MESH = pl.DeviceIdType.MESH


def near_first(count):
    order = []
    for step in range(1, count // 2 + 1):
        order.append(step)
        if count - step != step:
            order.append(count - step)
    return order


def greet(reps, layers):
    rep, place = lax.axis_index("rep"), lax.axis_index("fsdp")
    layer, lane = place // LANES, place % LANES
    barrier = pltpu.get_barrier_semaphore()
    for step in range(1, layers):
        peer = ((layer + step) % layers) * LANES + lane
        pl.semaphore_signal(barrier, inc=1, device_id=(rep, peer), device_id_type=MESH)
    for turn in range(reps):
        for hop in range(LANES):
            if turn or hop:
                peer = layer * LANES + (lane + hop) % LANES
                pl.semaphore_signal(
                    barrier, inc=1, device_id=((rep + turn) % reps, peer), device_id_type=MESH
                )
    pl.semaphore_wait(barrier, layers - 1 + reps * LANES - 1)


def exchange(reps, layers, send, mid, out, a_send, a_recv, b_send, b_recv, own):
    rep, place = lax.axis_index("rep"), lax.axis_index("fsdp")
    layer, lane = place // LANES, place % LANES
    first = []
    for step in near_first(layers)[::-1]:
        there = (layer + step) % layers
        copy = pltpu.make_async_remote_copy(
            src_ref=send.at[there],
            dst_ref=mid.at[:, layer],
            send_sem=a_send.at[step],
            recv_sem=a_recv.at[step],
            device_id=(rep, there * LANES + lane),
            device_id_type=MESH,
        )
        copy.start()
        first.append(copy)
    keep = pltpu.make_async_copy(send.at[layer], mid.at[:, layer], own.at[0])
    keep.start()
    keep.wait()
    for copy in first:
        copy.wait_recv()
    second = []
    for turn in (2, 1, 3, 0) if reps == 4 else range(reps):
        for hop in range(LANES):
            if turn or hop:
                target = (lane + hop) % LANES
                copy = pltpu.make_async_remote_copy(
                    src_ref=mid.at[target],
                    dst_ref=out.at[rep, :, lane],
                    send_sem=b_send.at[turn, hop],
                    recv_sem=b_recv.at[turn, hop],
                    device_id=((rep + turn) % reps, layer * LANES + target),
                    device_id_type=MESH,
                )
                copy.start()
                second.append(copy)
    stay = pltpu.make_async_copy(mid.at[lane], out.at[rep, :, lane], own.at[1])
    stay.start()
    stay.wait()
    for copy in second:
        copy.wait_recv()
    for copy in first + second:
        copy.wait_send()


def exchange_scratch(reps, layers, rows, width):
    return [
        pltpu.VMEM((LANES, layers, rows, width), jnp.bfloat16),
        pltpu.SemaphoreType.DMA((layers,)),
        pltpu.SemaphoreType.DMA((layers,)),
        pltpu.SemaphoreType.DMA((reps, LANES)),
        pltpu.SemaphoreType.DMA((reps, LANES)),
        pltpu.SemaphoreType.DMA((2,)),
    ]


def gather_kernel(
    reps, layers, grad, ids, out, parts, total, send, r_send, r_recv, r_own,
    mid, a_send, a_recv, b_send, b_recv, own,
):
    rep, place = lax.axis_index("rep"), lax.axis_index("fsdp")
    width = total.shape[-1]
    greet(reps, layers)
    copies = []
    for turn in range(1, reps):
        there = (rep + turn) % reps
        copy = pltpu.make_async_remote_copy(
            src_ref=grad.at[0, :, :, pl.ds(pl.multiple_of(there * width, width), width)],
            dst_ref=parts.at[turn],
            send_sem=r_send.at[turn],
            recv_sem=r_recv.at[turn],
            device_id=(there, place),
            device_id_type=MESH,
        )
        copy.start()
        copies.append(copy)
    mine = pltpu.make_async_copy(
        grad.at[0, :, :, pl.ds(pl.multiple_of(rep * width, width), width)], parts.at[0], r_own
    )
    mine.start()
    mine.wait()
    for copy in copies:
        copy.wait_recv()
    acc = parts[0].astype(jnp.float32)
    for turn in range(1, reps):
        acc = acc + parts[turn].astype(jnp.float32)
    total[...] = acc.astype(jnp.bfloat16)

    @pl.loop(0, layers)
    def _(layer):
        for lane in range(LANES):
            send[layer, lane] = total[ids[layer * LANES + lane]]

    exchange(reps, layers, send, mid, out, a_send, a_recv, b_send, b_recv, own)
    for copy in copies:
        copy.wait_send()


def return_kernel(reps, layers, piece, out, mid, a_send, a_recv, b_send, b_recv, own):
    greet(reps, layers)
    exchange(reps, layers, piece, mid, out, a_send, a_recv, b_send, b_recv, own)


def mm(a, b, dims=((1,), (0,))):
    return lax.dot_general(a, b, (dims, ((), ())), preferred_element_type=jnp.float32)


def root(stat):
    size = stat.shape[0]
    bound = jnp.max(jnp.sum(jnp.abs(stat), axis=0, keepdims=True))
    factor = 2.5 / bound
    row = lax.broadcasted_iota(jnp.int32, (size, size), 0)
    col = lax.broadcasted_iota(jnp.int32, (size, size), 1)
    step = jnp.where(row == col, 1.25, 0.0) - (0.25 * factor) * stat
    low = step.astype(jnp.bfloat16)
    square = mm(low, low)
    low2 = square.astype(jnp.bfloat16)
    fourth = mm(low2, low2).astype(jnp.bfloat16)
    inner = (5.0 * step - 4.0 * square).astype(jnp.bfloat16)
    gain = 0.25 * jnp.sqrt(jnp.sqrt(factor))
    return (gain * (5.0 * step - mm(fourth, inner))).astype(jnp.bfloat16)


def block_kernel(
    reps, blocks, left, right, live, left_out, right_out, piece, grad, left_new, right_new,
    shaped, sems,
):
    width = piece.shape[1]
    rep = lax.axis_index("rep")
    for part in range(reps):
        grad[:, part * width : (part + 1) * width] = blocks[part]
    g = grad[...]
    used = live[0] > 0
    gram_left = mm(g, g, ((1,), (1,)))
    left_new[...] = jnp.where(used, DECAY * left[0] + (1.0 - DECAY) * gram_left, left[0])
    put_left = pltpu.make_async_copy(left_new, left_out.at[0], sems.at[0])
    put_left.start()
    gram_right = mm(g, g, ((0,), (0,)))
    right_new[...] = jnp.where(used, DECAY * right[0] + (1.0 - DECAY) * gram_right, right[0])
    put_right = pltpu.make_async_copy(right_new, right_out.at[0], sems.at[1])
    put_right.start()
    left_root = root(left_new[...])
    right_root = root(right_new[...])
    half = mm(left_root, g).astype(jnp.bfloat16)
    shaped[...] = mm(half, right_root)
    wide = g.astype(jnp.float32)
    grad_norm = jnp.sqrt(jnp.sum(wide * wide))
    whole = shaped[...]
    shaped_norm = jnp.sqrt(jnp.sum(whole * whole) + 1e-06)
    scale = grad_norm / shaped_norm
    own = shaped[:, pl.ds(pl.multiple_of(rep * width, width), width)]
    piece[...] = (own * scale).astype(jnp.bfloat16)
    put_left.wait()
    put_right.wait()


def select_kernel(reps, workers, arrived, out):
    width = arrived.shape[-1]

    @pl.loop(0, out.shape[0] // 8)
    def _(group):
        for k in range(8):
            block = group * 8 + k
            worker = workers[block]
            for part in range(reps):
                out[block, :, part * width : (part + 1) * width] = arrived[part, worker]


def local(gradient, left_stats, right_stats, block_lists, block_counts):
    _, block_total, dev_rows, cols = gradient.shape
    reps, devices = lax.axis_size("rep"), lax.axis_size("fsdp")
    layers = devices // LANES
    width = cols // reps
    rows = devices * dev_rows
    vmem = pl.BlockSpec(memory_space=pltpu.VMEM)
    smem = pl.BlockSpec(memory_space=pltpu.SMEM)
    anywhere = pl.BlockSpec(memory_space=pl.ANY)

    live = block_counts > 0
    ids = jnp.clip(block_lists[:, 0], 0, block_total - 1)
    named = jnp.where(live, block_lists[:, 0], -1)
    place = jnp.arange(devices, dtype=jnp.int32)
    match = named[None, :] == jnp.arange(block_total, dtype=jnp.int32)[:, None]
    workers = jnp.sum(jnp.where(match, place[None, :], 0), axis=1)
    own_live = lax.dynamic_slice_in_dim(block_counts, lax.axis_index("fsdp"), 1)

    slots = jax.ShapeDtypeStruct((reps, layers, LANES, dev_rows, width), jnp.bfloat16)
    blocks = pl.pallas_call(
        functools.partial(gather_kernel, reps, layers),
        out_shape=slots,
        in_specs=[anywhere, smem],
        out_specs=anywhere,
        scratch_shapes=[
            pltpu.VMEM((reps, block_total, dev_rows, width), jnp.bfloat16),
            pltpu.VMEM((block_total, dev_rows, width), jnp.bfloat16),
            pltpu.VMEM((layers, LANES, dev_rows, width), jnp.bfloat16),
            pltpu.SemaphoreType.DMA((reps,)),
            pltpu.SemaphoreType.DMA((reps,)),
            pltpu.SemaphoreType.DMA(()),
        ]
        + exchange_scratch(reps, layers, dev_rows, width),
        compiler_params=pltpu.CompilerParams(
            collective_id=0, has_side_effects=True, vmem_limit_bytes=8 << 20
        ),
        name="gather_blocks",
    )(gradient, ids)

    left_new, right_new, piece = pl.pallas_call(
        functools.partial(block_kernel, reps),
        out_shape=(
            jax.ShapeDtypeStruct(left_stats.shape, jnp.float32),
            jax.ShapeDtypeStruct(right_stats.shape, jnp.float32),
            jax.ShapeDtypeStruct((rows, width), jnp.bfloat16),
        ),
        in_specs=[vmem, vmem, vmem, smem],
        out_specs=(anywhere, anywhere, vmem),
        scratch_shapes=[
            pltpu.VMEM((rows, cols), jnp.bfloat16),
            pltpu.VMEM((rows, rows), jnp.float32),
            pltpu.VMEM((cols, cols), jnp.float32),
            pltpu.VMEM((rows, cols), jnp.float32),
            pltpu.SemaphoreType.DMA((2,)),
        ],
        compiler_params=pltpu.CompilerParams(vmem_limit_bytes=32 << 20),
        name="precondition",
    )(blocks.reshape(reps, rows, width), left_stats, right_stats, own_live)

    arrived = pl.pallas_call(
        functools.partial(return_kernel, reps, layers),
        out_shape=slots,
        in_specs=[anywhere],
        out_specs=anywhere,
        scratch_shapes=exchange_scratch(reps, layers, dev_rows, width),
        compiler_params=pltpu.CompilerParams(
            collective_id=1, has_side_effects=True, vmem_limit_bytes=8 << 20
        ),
        name="return_rows",
    )(piece.reshape(layers, LANES, dev_rows, width))

    direction = pl.pallas_call(
        functools.partial(select_kernel, reps),
        out_shape=jax.ShapeDtypeStruct((block_total, dev_rows, cols), jnp.bfloat16),
        in_specs=[smem, vmem],
        out_specs=vmem,
        name="select_blocks",
    )(workers, arrived.reshape(reps, devices, dev_rows, width))
    return (direction, left_new, right_new)


def solution(mesh):
    placed = (P("rep", None, "fsdp", None), P("fsdp", None, None), P("fsdp", None, None), P(), P())
    return jax.shard_map(
        local,
        mesh=mesh,
        in_specs=placed,
        out_specs=(P(None, "fsdp", None), P("fsdp", None, None), P("fsdp", None, None)),
        check_vma=False,
    )
```

time: 219 us -> 75.6 us (0.35)
  waiting for transfers between devices: 119 us -> 0 us
  Pallas kernels: 0 us -> 68.4 us
  starting transfers between devices: 67.1 us -> 0 us
  between operations: 14.8 us -> 0.69 us
  local copies, waits for them, and re-layouts: 15.9 us -> 5.48 us
    pallas_call x0 -> x4, Pallas kernels: none -> 68.4 us  [the longest x1 38.6 us: local(): pl.pallas_call(functools.partial(gather_kernel, reps, layers), out_shape=...]
    all_to_all x2 -> x0, starting transfers between devices: 67.1 us -> none  [the longest x1 48.3 us: local(): lax.all_to_all(grafted.reshape(slot_count, workers, dev_rows, block_width...]
    psum x1 -> x0, waiting for transfers between devices: 62.7 us -> none  [local(): summed = lax.psum(own_rows.astype(jnp.bfloat16), 'rep')]
    all_to_all x2 -> x0, waiting for transfers between devices: 55.9 us -> none  [the longest x1 28.2 us: local(): lax.all_to_all(grafted.reshape(slot_count, workers, dev_rows, block_width...]
    scatter x1 -> x0, local copies, waits for them, and re-layouts: 4.47 us -> none  [local(): direction = jnp.zeros((block_total, dev_rows, block_width), jnp.bfloat16)...]
    gather x1 -> x0, local copies, waits for them, and re-layouts: 2.74 us -> none  [local(): outgoing = summed[safe_ids.T]]
    cond x2 -> x0, local copies, waits for them, and re-layouts: 2.61 us -> none  [one_slot(): lax.cond(usable, precondition, skip_slot, grad_block, left_stat, right_stat)]
    unnamed x10 -> x12, local copies, waits for them, and re-layouts: 2.6 us -> 4.89 us
  transfers between devices with their start and end apart: 3 -> 0, of which waited for: 3 -> 0; matrix products, arithmetic and copies ran while one was open for 2% -> 0% of each run, Pallas kernels for 0% -> 0%
where the time goes in v1:
time: 75.6 us; the launch traced here: 75.3 us
  Pallas kernels  68.4 us (90%)
  local copies, waits for them, and re-layouts  5.48 us (7%)
    pallas_call x1, Pallas kernels, local(): pl.pallas_call(functools.partial(gather_kernel, reps, layers), out_shape=...  38.6 us
    pallas_call x1, Pallas kernels, local(): pl.pallas_call(functools.partial(return_kernel, reps, layers), out_shape=...  23.3 us
    unnamed x12, local copies, waits for them, and re-layouts  4.89 us
    pallas_call x1, Pallas kernels, local(): pl.pallas_call(functools.partial(block_kernel, reps), out_shape=(jax.Shap...  4.57 us
    pallas_call x1, Pallas kernels, local(): pl.pallas_call(functools.partial(select_kernel, reps), out_shape=jax.Shap...  1.93 us

profile of v1, /device:TPU:1, one launch (start us, length us, event | category | flops | bytes accessed | tf_op | source)
XLA Modules:
  0.0 75.3 jit_solution(4558092594993309021)
XLA Ops:
  0.6 0.0 copy-start.5
  0.6 0.6 copy-done.5
  1.3 0.0 copy-start.4
  1.3 0.6 dynamic_slice.3.live
  1.9 0.1 copy-done.4
  2.0 0.7 select_reduce_fusion.workers
  2.6 0.0 copy-start.3
  2.6 0.9 %copy-done.3 = bf16[1,64,4,512]{3,2,1,0:T(4,128)(2,1)S(1)} copy-done((bf16[1,64,4,512]{3,2,1,0:T(4,128)(2,1)S(1)}, bf16[1,64,4,512]{3,2,1,0:T(4,128)(2,1)}, u32[]{:S(2)}) %copy-start.3) | copy-done | bytes 262168
  3.6 38.6 %gather_blocks.1 = bf16[4,16,8,4,128]{4,3,2,1,0:T(4,128)(2,1)S(1)} custom-call(bf16[1,64,4,512]{3,2,1,0:T(4,128)(2,1)S(1)} %copy-done.3, s32[128]{0:T(128)S(1)} %get-tuple-element.9.ids), custom_call_target="tpu_custom_call" | custom-call | tf_op jit(solution)/shard_map/gather_blocks/pallas_call | solution.py:228
  42.2 0.0 copy-start.1
  42.2 1.2 %copy-done.1 = f32[1,512,512]{2,1,0:T(8,128)S(1)} copy-done((f32[1,512,512]{2,1,0:T(8,128)S(1)}, f32[1,512,512]{2,1,0:T(8,128)}, u32[]{:S(2)}) %copy-start.1) | copy-done | bytes 1048600
  43.4 0.0 copy-start.2
  43.4 1.2 %copy-done.2 = f32[1,512,512]{2,1,0:T(8,128)S(1)} copy-done((f32[1,512,512]{2,1,0:T(8,128)S(1)}, f32[1,512,512]{2,1,0:T(8,128)}, u32[]{:S(2)}) %copy-start.2) | copy-done | bytes 1048600
  44.7 4.6 %precondition.1 = (f32[1,512,512]{2,1,0:T(8,128)}, f32[1,512,512]{2,1,0:T(8,128)}, bf16[512,128]{1,0:T(8,128)(2,1)S(1)}) custom-call(bf16[4,512,128]{2,1,0:T(8,128)(2,1)S(1)} %bitcast.7, f32[1,512,512]{2,1,0:T(8,128)S(1)} %copy-done.1, f32[1,512,512]{2,1,0:T(8,128)S(1)} %copy-done.2, s32[1]{0:T(128)} %dynamic_slice.3.live), custom_call_target="tpu_custom_call" | custom-call | tf_op jit(solution)/shard_map/precondition/pallas_call | solution.py:248
  49.2 23.3 %return_rows.1 = bf16[4,16,8,4,128]{4,3,2,1,0:T(4,128)(2,1)S(1)} custom-call(bf16[16,8,4,128]{3,2,1,0:T(4,128)(2,1)S(1)} %bitcast.8), custom_call_target="tpu_custom_call" | custom-call | tf_op jit(solution)/shard_map/return_rows/pallas_call | solution.py:268
  72.6 0.0 copy-start
  72.6 0.8 %copy-done = bf16[4,16,8,4,128]{4,3,2,1,0:T(4,128)(2,1)} copy-done((bf16[4,16,8,4,128]{4,3,2,1,0:T(4,128)(2,1)}, bf16[4,16,8,4,128]{4,3,2,1,0:T(4,128)(2,1)S(1)}, u32[]{:S(2)}) %copy-start) | copy-done | bytes 524312
  73.4 1.9 %select_blocks.1 = bf16[64,4,512]{2,1,0:T(4,128)(2,1)} custom-call(s32[64]{0:T(128)} %select_reduce_fusion.workers, bf16[4,128,4,128]{3,2,1,0:T(4,128)(2,1)} %bitcast.6), custom_call_target="tpu_custom_call" | custom-call | tf_op jit(solution)/shard_map/select_blocks/pallas_call | solution.py:280
  (1 shorter events, 0.0 us)
Async XLA Ops:
  0.6 0.7 copy-start.5
  1.3 0.7 copy-start.4
  2.6 0.9 %copy-start.3 = (bf16[1,64,4,512]{3,2,1,0:T(4,128)(2,1)S(1)}, bf16[1,64,4,512]{3,2,1,0:T(4,128)(2,1)}, u32[]{:S(2)}) copy-start(bf16[1,64,4,512]{3,2,1,0:T(4,128)(2,1)} %grad.1) | copy-start | bytes 786436
  42.2 1.2 %copy-start.1 = (f32[1,512,512]{2,1,0:T(8,128)S(1)}, f32[1,512,512]{2,1,0:T(8,128)}, u32[]{:S(2)}) copy-start(f32[1,512,512]{2,1,0:T(8,128)} %left.1) | copy-start | bytes 3145732
  43.4 1.2 %copy-start.2 = (f32[1,512,512]{2,1,0:T(8,128)S(1)}, f32[1,512,512]{2,1,0:T(8,128)}, u32[]{:S(2)}) copy-start(f32[1,512,512]{2,1,0:T(8,128)} %right.1) | copy-start | bytes 3145732
  72.6 0.8 %copy-start = (bf16[4,16,8,4,128]{4,3,2,1,0:T(4,128)(2,1)}, bf16[4,16,8,4,128]{4,3,2,1,0:T(4,128)(2,1)S(1)}, u32[]{:S(2)}) copy-start(bf16[4,16,8,4,128]{4,3,2,1,0:T(4,128)(2,1)S(1)} %return_rows.1) | copy-start | bytes 1572868

commit v2 on v0

v2 whole, which is shorter than its diff:
```python
import functools

import jax
import jax.numpy as jnp
from jax import lax
from jax.experimental import pallas as pl
from jax.experimental.pallas import tpu as pltpu
from jax.sharding import PartitionSpec as P

DECAY = 0.95
LANES = 8
MESH = pl.DeviceIdType.MESH
PIECES = 4


def near_first(count):
    order = [0]
    for step in range(1, count // 2 + 1):
        order.append(step)
        if count - step != step:
            order.append(count - step)
    return order


def groups_of(layers):
    cuts = [0, layers]
    return [(lo, hi) for lo, hi in zip(cuts, cuts[1:]) if hi > lo]


def position():
    rep, place = lax.axis_index("rep"), lax.axis_index("fsdp")
    return rep, place, place // LANES, place % LANES


def reach_of(layers):
    return (layers // 2 + 1) // 2


def greet(reps, layers, relay):
    rep, place, layer, lane = position()
    reach = reach_of(layers)
    barrier = pltpu.get_barrier_semaphore()
    peers = []
    for step in range(reach, 0, -1):
        for way in (step, layers - step):
            peers.append((rep, ((layer + way) % layers) * LANES + lane))
    peers += [((rep + turn) % reps, place) for turn in range(1, reps)]
    peers += [(rep, layer * LANES + (lane + hop) % LANES) for hop in range(1, LANES)]
    for peer in peers:
        pl.semaphore_signal(barrier, inc=1, device_id=peer, device_id_type=MESH)
    pl.semaphore_wait(barrier, len(peers))
    for way in (reach, layers - reach):
        there = ((layer + way) % layers) * LANES + lane
        pl.semaphore_signal(relay, inc=1, device_id=(rep, there), device_id_type=MESH)


def take(ref, sem):
    pltpu.make_async_copy(ref, ref, sem).wait()


def exchange(reps, layers, send, mid, out, a_send, a_recv, b_send, b_recv):
    rep, _, layer, lane = position()
    order = near_first(layers)
    groups = groups_of(layers)
    for slot in range(layers - 1, 0, -1):
        there = (layer - order[slot] + layers) % layers
        group = [lo <= slot < hi for lo, hi in groups].index(True)
        pltpu.make_async_remote_copy(
            src_ref=send.at[there],
            dst_ref=mid.at[:, slot],
            send_sem=a_send,
            recv_sem=a_recv.at[group],
            device_id=(rep, there * LANES + lane),
            device_id_type=MESH,
        ).start()
    mid[:, 0] = send[layer]
    for group, (lo, hi) in enumerate(groups):
        if max(lo, 1) < hi:
            take(mid.at[:, max(lo, 1) : hi], a_recv.at[group])
        for turn in [t for t in (2, 1, 3) if t < reps] + [0]:
            for hop in (4, 3, 5, 2, 6, 1, 7, 0):
                if turn or hop:
                    target = (lane + hop) % LANES
                    pltpu.make_async_remote_copy(
                        src_ref=mid.at[target, lo:hi],
                        dst_ref=out.at[rep, lo:hi, lane],
                        send_sem=b_send.at[min(turn, 1)],
                        recv_sem=b_recv.at[min(turn, 1)],
                        device_id=((rep + turn) % reps, layer * LANES + target),
                        device_id_type=MESH,
                    ).start()
    out[rep, :, lane] = mid[lane]
    take(out.at[0 : reps - 1], b_recv.at[1])
    take(out.at[0, 0 : layers - layers // LANES], b_recv.at[0])


def exchange_end(reps, layers, mid, out, a_send, b_send):
    take(mid.at[:, 1:], a_send)
    take(out.at[0 : reps - 1], b_send.at[1])
    take(out.at[0, 0 : layers - layers // LANES], b_send.at[0])


def mm(a, b, dims=((1,), (0,))):
    return lax.dot_general(a, b, (dims, ((), ())), preferred_element_type=jnp.float32)


def root(stat):
    size = stat.shape[0]
    bound = jnp.max(jnp.sum(jnp.abs(stat), axis=0, keepdims=True))
    factor = 2.5 / bound
    row = lax.broadcasted_iota(jnp.int32, (size, size), 0)
    col = lax.broadcasted_iota(jnp.int32, (size, size), 1)
    diagonal = row == col
    d = jnp.where(diagonal, 0.25, 0.0) - (0.25 * factor) * stat
    low = d.astype(jnp.bfloat16)
    e = 2.0 * d + mm(low, low)
    low = e.astype(jnp.bfloat16)
    k = 2.0 * e + mm(low, low)
    j = 5.0 * d - 4.0 * e
    kj = mm(k.astype(jnp.bfloat16), j.astype(jnp.bfloat16))
    gain = jnp.sqrt(jnp.sqrt(factor))
    return (gain * (jnp.where(diagonal, 1.0, 0.0) + e - 0.25 * (k + kj))).astype(jnp.bfloat16)


def kernel(
    reps, layers, grad, ids_in, counts_in, left, right,
    direction, left_out, right_out,
    parts, total, send, mid_in, blocks, g_ref, stat_left, stat_right, left_new, right_new, shaped,
    piece, mid_out, arrived, table, table_smem, ids, counts, ids_row, counts_row,
    relay, r_send, r_recv, r_own, small_sems, stat_sems, put_sems, table_sem,
    a_send, a_recv, b_send, b_recv, c_send, c_recv, d_send, d_recv,
):
    rep, place, layer, lane = position()
    block_total, dev_rows, width = total.shape
    rows = LANES * dev_rows
    greet(reps, layers, relay)

    for turn in [t for t in (2, 1, 3) if t < reps]:
        there = (rep + turn) % reps
        pltpu.make_async_remote_copy(
            src_ref=grad.at[0, :, :, pl.ds(pl.multiple_of(there * width, width), width)],
            dst_ref=parts.at[turn],
            send_sem=r_send,
            recv_sem=r_recv,
            device_id=(there, place),
            device_id_type=MESH,
        ).start()

    mine = pltpu.make_async_copy(
        grad.at[0, :, :, pl.ds(pl.multiple_of(rep * width, width), width)], parts.at[0], r_own
    )
    small = [
        pltpu.make_async_copy(ids_in, ids, small_sems.at[0]),
        pltpu.make_async_copy(counts_in, counts, small_sems.at[1]),
        pltpu.make_async_copy(ids_in, ids_row, small_sems.at[2]),
        pltpu.make_async_copy(counts_in, counts_row, small_sems.at[3]),
    ]
    get_left = pltpu.make_async_copy(left.at[0], stat_left, stat_sems.at[0])
    get_right = pltpu.make_async_copy(right.at[0], stat_right, stat_sems.at[1])
    for copy in (mine, *small, get_left, get_right):
        copy.start()
    for copy in small:
        copy.wait()

    devices = layers * LANES
    worker = lax.broadcasted_iota(jnp.int32, (devices, devices), 0)
    named = jnp.where(counts_row[...] > 0, ids_row[...], -1)
    named = jnp.transpose(jnp.broadcast_to(named, (devices, devices)))
    match = named == lax.broadcasted_iota(jnp.int32, (devices, devices), 1)
    offset = (worker // LANES - layer + layers) % layers
    slot = jnp.where(offset <= layers // 2, jnp.maximum(2 * offset - 1, 0), 2 * (layers - offset))
    spot = slot * LANES + worker % LANES
    table[...] = jnp.max(jnp.where(match, spot, 0), axis=0, keepdims=True)
    put_table = pltpu.make_async_copy(table, table_smem, table_sem)
    put_table.start()

    mine.wait()
    take(parts.at[1:reps], r_recv)
    acc = parts[0].astype(jnp.float32)
    for turn in range(1, reps):
        acc = acc + parts[turn].astype(jnp.float32)
    total[...] = acc.astype(jnp.bfloat16)

    @pl.loop(0, layers)
    def _(z):
        for l in range(LANES):
            block = jnp.clip(ids[0, z * LANES + l], 0, block_total - 1)
            send[z, l] = total[block]

    pl.semaphore_wait(relay, 2)
    exchange(reps, layers, send, mid_in, blocks, a_send, a_recv, b_send, b_recv)

    for part in range(reps):
        for slot_at, offset_at in enumerate(near_first(layers)):
            start = pl.multiple_of(((layer + offset_at) % layers) * rows, rows)
            g_ref[pl.ds(start, rows), part * width : (part + 1) * width] = blocks[
                part, slot_at
            ].reshape(rows, width)
    g = g_ref[...]
    used = counts[0, place] > 0
    get_left.wait()
    get_right.wait()
    old = stat_left[...]
    left_new[...] = jnp.where(used, DECAY * old + (1.0 - DECAY) * mm(g, g, ((1,), (1,))), old)
    put_left = pltpu.make_async_copy(left_new, left_out.at[0], put_sems.at[0])
    put_left.start()
    old = stat_right[...]
    right_new[...] = jnp.where(used, DECAY * old + (1.0 - DECAY) * mm(g, g, ((0,), (0,))), old)
    put_right = pltpu.make_async_copy(right_new, right_out.at[0], put_sems.at[1])
    put_right.start()
    left_root = root(left_new[...])
    right_root = root(right_new[...])
    half = mm(left_root, g).astype(jnp.bfloat16)
    shaped[...] = mm(half, right_root)
    wide = g.astype(jnp.float32)
    grad_norm = jnp.sqrt(jnp.sum(wide * wide))
    whole = shaped[...]
    shaped_norm = jnp.sqrt(jnp.sum(whole * whole) + 1e-06)
    own = shaped[:, pl.ds(pl.multiple_of(rep * width, width), width)]
    grafted = (own * (grad_norm / shaped_norm)).astype(jnp.bfloat16)
    piece[...] = grafted.reshape(piece.shape)

    exchange(reps, layers, piece, mid_out, arrived, c_send, c_recv, d_send, d_recv)
    put_table.wait()

    @pl.loop(0, block_total // 8)
    def _(group):
        for k in range(8):
            block = group * 8 + k
            spot_at = table_smem[0, block]
            for part in range(reps):
                direction[block, :, part * width : (part + 1) * width] = arrived[
                    part, spot_at // LANES, spot_at % LANES
                ]

    take(parts.at[1:reps], r_send)
    exchange_end(reps, layers, mid_in, blocks, a_send, b_send)
    exchange_end(reps, layers, mid_out, arrived, c_send, d_send)
    put_left.wait()
    put_right.wait()


def hand_over(direction, left, right, direction_out, left_out, right_out, a, b, c, get_sems, put_sems):
    moves = []
    for k, (src, via, dst) in enumerate(
        [(left.at[0], a, left_out.at[0]), (right.at[0], b, right_out.at[0]), (direction, c, direction_out)]
    ):
        step = src.shape[0] // PIECES
        for p in range(PIECES):
            span = pl.ds(p * step, step)
            moves.append(
                (
                    pltpu.make_async_copy(src.at[span], via.at[span], get_sems.at[k, p]),
                    pltpu.make_async_copy(via.at[span], dst.at[span], put_sems.at[k, p]),
                )
            )
    for get, _ in moves:
        get.start()
    for get, put in moves:
        get.wait()
        put.start()
    for _, put in moves:
        put.wait()


def local(gradient, left_stats, right_stats, block_lists, block_counts):
    _, block_total, dev_rows, cols = gradient.shape
    reps, devices = lax.axis_size("rep"), lax.axis_size("fsdp")
    layers = devices // LANES
    width = cols // reps
    rows = devices * dev_rows
    vmem = pl.BlockSpec(memory_space=pltpu.VMEM)
    anywhere = pl.BlockSpec(memory_space=pl.ANY)
    groups = len(groups_of(layers))
    direction, left_new, right_new = pl.pallas_call(
        functools.partial(kernel, reps, layers),
        out_shape=(
            jax.ShapeDtypeStruct((block_total, dev_rows, cols), jnp.bfloat16),
            jax.ShapeDtypeStruct(left_stats.shape, jnp.float32),
            jax.ShapeDtypeStruct(right_stats.shape, jnp.float32),
        ),
        in_specs=[anywhere] * 5,
        out_specs=(vmem, anywhere, anywhere),
        scratch_shapes=[
            pltpu.VMEM((reps, block_total, dev_rows, width), jnp.bfloat16),
            pltpu.VMEM((block_total, dev_rows, width), jnp.bfloat16),
            pltpu.VMEM((layers, LANES, dev_rows, width), jnp.bfloat16),
            pltpu.VMEM((LANES, layers, dev_rows, width), jnp.bfloat16),
            pltpu.VMEM((reps, layers, LANES, dev_rows, width), jnp.bfloat16),
            pltpu.VMEM((rows, cols), jnp.bfloat16),
            pltpu.VMEM((rows, rows), jnp.float32),
            pltpu.VMEM((cols, cols), jnp.float32),
            pltpu.VMEM((rows, rows), jnp.float32),
            pltpu.VMEM((cols, cols), jnp.float32),
            pltpu.VMEM((rows, cols), jnp.float32),
            pltpu.VMEM((layers, LANES, dev_rows, width), jnp.bfloat16),
            pltpu.VMEM((LANES, layers, dev_rows, width), jnp.bfloat16),
            pltpu.VMEM((reps, layers, LANES, dev_rows, width), jnp.bfloat16),
            pltpu.VMEM((1, devices), jnp.int32),
            pltpu.SMEM((1, devices), jnp.int32),
            pltpu.SMEM((1, devices), jnp.int32),
            pltpu.SMEM((1, devices), jnp.int32),
            pltpu.VMEM((1, devices), jnp.int32),
            pltpu.VMEM((1, devices), jnp.int32),
            pltpu.SemaphoreType.REGULAR,
            pltpu.SemaphoreType.DMA(()),
            pltpu.SemaphoreType.DMA(()),
            pltpu.SemaphoreType.DMA(()),
            pltpu.SemaphoreType.DMA((4,)),
            pltpu.SemaphoreType.DMA((2,)),
            pltpu.SemaphoreType.DMA((2,)),
            pltpu.SemaphoreType.DMA(()),
        ]
        + 2
        * [
            pltpu.SemaphoreType.DMA(()),
            pltpu.SemaphoreType.DMA((groups,)),
            pltpu.SemaphoreType.DMA((2,)),
            pltpu.SemaphoreType.DMA((2,)),
        ],
        compiler_params=pltpu.CompilerParams(
            collective_id=0, has_side_effects=True, vmem_limit_bytes=63 << 20
        ),
        name="shampoo_step",
    )(
        gradient, block_lists.reshape(1, devices), block_counts.reshape(1, devices),
        left_stats, right_stats,
    )
    results = (direction, left_new, right_new)
    return pl.pallas_call(
        hand_over,
        out_shape=tuple(jax.ShapeDtypeStruct(x.shape, x.dtype) for x in results),
        in_specs=[anywhere] * 3,
        out_specs=(anywhere,) * 3,
        scratch_shapes=[
            pltpu.VMEM(left_stats.shape[1:], jnp.float32),
            pltpu.VMEM(right_stats.shape[1:], jnp.float32),
            pltpu.VMEM(direction.shape, jnp.bfloat16),
            pltpu.SemaphoreType.DMA((3, PIECES)),
            pltpu.SemaphoreType.DMA((3, PIECES)),
        ],
        compiler_params=pltpu.CompilerParams(vmem_limit_bytes=63 << 20),
        name="hand_over",
    )(*results)


def solution(mesh):
    placed = (P("rep", None, "fsdp", None), P("fsdp", None, None), P("fsdp", None, None), P(), P())
    return jax.shard_map(
        local,
        mesh=mesh,
        in_specs=placed,
        out_specs=(P(None, "fsdp", None), P("fsdp", None, None), P("fsdp", None, None)),
        check_vma=False,
    )
```

time: 219 us -> 60.6 us (0.28)
  waiting for transfers between devices: 119 us -> 0 us
  starting transfers between devices: 67.1 us -> 0 us
  Pallas kernels: 0 us -> 59.8 us
  local copies, waits for them, and re-layouts: 15.9 us -> 0 us
  between operations: 14.8 us -> 0.64 us
    all_to_all x2 -> x0, starting transfers between devices: 67.1 us -> none  [the longest x1 48.3 us: local(): lax.all_to_all(grafted.reshape(slot_count, workers, dev_rows, block_width...]
    psum x1 -> x0, waiting for transfers between devices: 62.7 us -> none  [local(): summed = lax.psum(own_rows.astype(jnp.bfloat16), 'rep')]
    pallas_call x0 -> x2, Pallas kernels: none -> 59.8 us  [the longest x1 57.3 us: local(): pl.pallas_call(functools.partial(kernel, reps, layers), out_shape=(jax.Sh...]
    all_to_all x2 -> x0, waiting for transfers between devices: 55.9 us -> none  [the longest x1 28.2 us: local(): lax.all_to_all(grafted.reshape(slot_count, workers, dev_rows, block_width...]
    scatter x1 -> x0, local copies, waits for them, and re-layouts: 4.47 us -> none  [local(): direction = jnp.zeros((block_total, dev_rows, block_width), jnp.bfloat16)...]
    gather x1 -> x0, local copies, waits for them, and re-layouts: 2.74 us -> none  [local(): outgoing = summed[safe_ids.T]]
    cond x2 -> x0, local copies, waits for them, and re-layouts: 2.61 us -> none  [one_slot(): lax.cond(usable, precondition, skip_slot, grad_block, left_stat, right_stat)]
    unnamed x10 -> x0, local copies, waits for them, and re-layouts: 2.6 us -> none
  transfers between devices with their start and end apart: 3 -> 0, of which waited for: 3 -> 0; matrix products, arithmetic and copies ran while one was open for 2% -> 0% of each run, Pallas kernels for 0% -> 0%
where the time goes in v2:
time: 60.6 us; the launch traced here: 60.5 us
  Pallas kernels  59.8 us (99%)
  between operations  0.64 us (1%)
    pallas_call x1, Pallas kernels, local(): pl.pallas_call(functools.partial(kernel, reps, layers), out_shape=(jax.Sh...  57.3 us
    pallas_call x1, Pallas kernels, local(): pl.pallas_call(hand_over, out_shape=tuple((jax.ShapeDtypeStruct(x.shape,...  2.54 us

profile of v2, /device:TPU:1, one launch (start us, length us, event | category | flops | bytes accessed | tf_op | source)
XLA Modules:
  0.0 60.5 jit_solution(17417046071727262134)
XLA Ops:
  0.6 57.3 %shampoo_step.1 = (bf16[64,4,512]{2,1,0:T(4,128)(2,1)}, f32[1,512,512]{2,1,0:T(8,128)}, f32[1,512,512]{2,1,0:T(8,128)}) custom-call(bf16[1,64,4,512]{3,2,1,0:T(4,128)(2,1)} %grad.1, s32[1,128]{1,0:T(1,128)} %bitcast.2, s32[1,128]{1,0:T(1,128)} %bitcast.3, f32[1,512,512]{2,1,0:T(8,128)} %left.1, f32[1,512,512]{2,1,0:T(8,128)} %right.1), custom_call_target="tpu_custom_call" | custom-call | tf_op jit(solution)/shard_map/shampoo_step/pallas_call | solution.py:275
  57.9 2.5 %hand_over.1 = (bf16[64,4,512]{2,1,0:T(4,128)(2,1)}, f32[1,512,512]{2,1,0:T(8,128)}, f32[1,512,512]{2,1,0:T(8,128)}) custom-call(bf16[64,4,512]{2,1,0:T(4,128)(2,1)} %get-tuple-element.6.direction, f32[1,512,512]{2,1,0:T(8,128)} %get-tuple-element.7.left, f32[1,512,512]{2,1,0:T(8,128)} %get-tuple-element.8.right), custom_call_target="tpu_custom_call" | custom-call | tf_op jit(solution)/shard_map/hand_over/pallas_call | solution.py:330

commit v3 on v2

--- a/solution.py
+++ b/solution.py
@@ -10,7 +10,8 @@
 DECAY = 0.95
 LANES = 8
 MESH = pl.DeviceIdType.MESH
-PIECES = 4
+PIECES = 2
+GROUPS = 4
 
 
 def near_first(count):
@@ -22,9 +23,9 @@
     return order
 
 
-def groups_of(layers):
-    cuts = [0, layers]
-    return [(lo, hi) for lo, hi in zip(cuts, cuts[1:]) if hi > lo]
+def groups_of(layers, cuts):
+    ends = [0] + [cut * layers // 16 for cut in cuts] + [layers]
+    return [(lo, hi) for lo, hi in zip(ends, ends[1:]) if hi > lo]
 
 
 def position():
@@ -58,11 +59,11 @@
     pltpu.make_async_copy(ref, ref, sem).wait()
 
 
-def exchange(reps, layers, send, mid, out, a_send, a_recv, b_send, b_recv):
+def exchange(reps, layers, cuts, send, mid, out, a_send, a_recv, b_send, b_recv):
     rep, _, layer, lane = position()
     order = near_first(layers)
-    groups = groups_of(layers)
-    for slot in range(layers - 1, 0, -1):
+    groups = groups_of(layers, cuts)
+    for slot in range(1, layers) if cuts else range(layers - 1, 0, -1):
         there = (layer - order[slot] + layers) % layers
         group = [lo <= slot < hi for lo, hi in groups].index(True)
         pltpu.make_async_remote_copy(
@@ -125,20 +126,30 @@
 def kernel(
     reps, layers, grad, ids_in, counts_in, left, right,
     direction, left_out, right_out,
-    parts, total, send, mid_in, blocks, g_ref, stat_left, stat_right, left_new, right_new, shaped,
+    local, parts, total, send, mid_in, blocks, g_ref, stat_left, stat_right, left_new, right_new, shaped,
     piece, mid_out, arrived, table, table_smem, ids, counts, ids_row, counts_row,
-    relay, r_send, r_recv, r_own, small_sems, stat_sems, put_sems, table_sem,
+    relay, r_send, r_recv, fetch_sems, small_sems, stat_sems, put_sems, table_sem,
     a_send, a_recv, b_send, b_recv, c_send, c_recv, d_send, d_recv,
 ):
     rep, place, layer, lane = position()
     block_total, dev_rows, width = total.shape
     rows = LANES * dev_rows
+    fetch = []
+    for part in range(reps):
+        fetch.append(
+            pltpu.make_async_copy(
+                grad.at[0, :, :, part * width : (part + 1) * width], local.at[part], fetch_sems.at[part]
+            )
+        )
+        fetch[-1].start()
     greet(reps, layers, relay)
+    for copy in fetch:
+        copy.wait()
 
     for turn in [t for t in (2, 1, 3) if t < reps]:
         there = (rep + turn) % reps
         pltpu.make_async_remote_copy(
-            src_ref=grad.at[0, :, :, pl.ds(pl.multiple_of(there * width, width), width)],
+            src_ref=local.at[there],
             dst_ref=parts.at[turn],
             send_sem=r_send,
             recv_sem=r_recv,
@@ -146,9 +157,6 @@
             device_id_type=MESH,
         ).start()
 
-    mine = pltpu.make_async_copy(
-        grad.at[0, :, :, pl.ds(pl.multiple_of(rep * width, width), width)], parts.at[0], r_own
-    )
     small = [
         pltpu.make_async_copy(ids_in, ids, small_sems.at[0]),
         pltpu.make_async_copy(counts_in, counts, small_sems.at[1]),
@@ -157,7 +165,7 @@
     ]
     get_left = pltpu.make_async_copy(left.at[0], stat_left, stat_sems.at[0])
     get_right = pltpu.make_async_copy(right.at[0], stat_right, stat_sems.at[1])
-    for copy in (mine, *small, get_left, get_right):
+    for copy in (*small, get_left, get_right):
         copy.start()
     for copy in small:
         copy.wait()
@@ -174,9 +182,8 @@
     put_table = pltpu.make_async_copy(table, table_smem, table_sem)
     put_table.start()
 
-    mine.wait()
     take(parts.at[1:reps], r_recv)
-    acc = parts[0].astype(jnp.float32)
+    acc = local[rep].astype(jnp.float32)
     for turn in range(1, reps):
         acc = acc + parts[turn].astype(jnp.float32)
     total[...] = acc.astype(jnp.bfloat16)
@@ -188,7 +195,7 @@
             send[z, l] = total[block]
 
     pl.semaphore_wait(relay, 2)
-    exchange(reps, layers, send, mid_in, blocks, a_send, a_recv, b_send, b_recv)
+    exchange(reps, layers, (), send, mid_in, blocks, a_send, a_recv, b_send, b_recv)
 
     for part in range(reps):
         for slot_at, offset_at in enumerate(near_first(layers)):
@@ -202,12 +209,10 @@
     get_right.wait()
     old = stat_left[...]
     left_new[...] = jnp.where(used, DECAY * old + (1.0 - DECAY) * mm(g, g, ((1,), (1,))), old)
-    put_left = pltpu.make_async_copy(left_new, left_out.at[0], put_sems.at[0])
-    put_left.start()
+    left_out[0] = left_new[...]
     old = stat_right[...]
     right_new[...] = jnp.where(used, DECAY * old + (1.0 - DECAY) * mm(g, g, ((0,), (0,))), old)
-    put_right = pltpu.make_async_copy(right_new, right_out.at[0], put_sems.at[1])
-    put_right.start()
+    right_out[0] = right_new[...]
     left_root = root(left_new[...])
     right_root = root(right_new[...])
     half = mm(left_root, g).astype(jnp.bfloat16)
@@ -220,7 +225,7 @@
     grafted = (own * (grad_norm / shaped_norm)).astype(jnp.bfloat16)
     piece[...] = grafted.reshape(piece.shape)
 
-    exchange(reps, layers, piece, mid_out, arrived, c_send, c_recv, d_send, d_recv)
+    exchange(reps, layers, (7,), piece, mid_out, arrived, c_send, c_recv, d_send, d_recv)
     put_table.wait()
 
     @pl.loop(0, block_total // 8)
@@ -236,31 +241,21 @@
     take(parts.at[1:reps], r_send)
     exchange_end(reps, layers, mid_in, blocks, a_send, b_send)
     exchange_end(reps, layers, mid_out, arrived, c_send, d_send)
-    put_left.wait()
-    put_right.wait()
-
-
-def hand_over(direction, left, right, direction_out, left_out, right_out, a, b, c, get_sems, put_sems):
-    moves = []
-    for k, (src, via, dst) in enumerate(
-        [(left.at[0], a, left_out.at[0]), (right.at[0], b, right_out.at[0]), (direction, c, direction_out)]
+
+
+def hand_over(direction, left, right, direction_out, left_out, right_out, sems):
+    copies = []
+    for k, (src, dst) in enumerate(
+        [(left.at[0], left_out.at[0]), (right.at[0], right_out.at[0]), (direction, direction_out)]
     ):
         step = src.shape[0] // PIECES
         for p in range(PIECES):
             span = pl.ds(p * step, step)
-            moves.append(
-                (
-                    pltpu.make_async_copy(src.at[span], via.at[span], get_sems.at[k, p]),
-                    pltpu.make_async_copy(via.at[span], dst.at[span], put_sems.at[k, p]),
-                )
-            )
-    for get, _ in moves:
-        get.start()
-    for get, put in moves:
-        get.wait()
-        put.start()
-    for _, put in moves:
-        put.wait()
+            copies.append(pltpu.make_async_copy(src.at[span], dst.at[span], sems.at[k, p]))
+    for copy in copies:
+        copy.start()
+    for copy in copies:
+        copy.wait()
 
 
 def local(gradient, left_stats, right_stats, block_lists, block_counts):
@@ -271,17 +266,20 @@
     rows = devices * dev_rows
     vmem = pl.BlockSpec(memory_space=pltpu.VMEM)
     anywhere = pl.BlockSpec(memory_space=pl.ANY)
-    groups = len(groups_of(layers))
+    def keep(x):
+        return pltpu.with_memory_space_constraint(x, pltpu.HBM)
+
     direction, left_new, right_new = pl.pallas_call(
         functools.partial(kernel, reps, layers),
         out_shape=(
-            jax.ShapeDtypeStruct((block_total, dev_rows, cols), jnp.bfloat16),
-            jax.ShapeDtypeStruct(left_stats.shape, jnp.float32),
-            jax.ShapeDtypeStruct(right_stats.shape, jnp.float32),
+            pltpu.VMEM((block_total, dev_rows, cols), jnp.bfloat16),
+            pltpu.VMEM(left_stats.shape, jnp.float32),
+            pltpu.VMEM(right_stats.shape, jnp.float32),
         ),
         in_specs=[anywhere] * 5,
-        out_specs=(vmem, anywhere, anywhere),
+        out_specs=(vmem, vmem, vmem),
         scratch_shapes=[
+            pltpu.VMEM((reps, block_total, dev_rows, width), jnp.bfloat16),
             pltpu.VMEM((reps, block_total, dev_rows, width), jnp.bfloat16),
             pltpu.VMEM((block_total, dev_rows, width), jnp.bfloat16),
             pltpu.VMEM((layers, LANES, dev_rows, width), jnp.bfloat16),
@@ -305,7 +303,7 @@
             pltpu.SemaphoreType.REGULAR,
             pltpu.SemaphoreType.DMA(()),
             pltpu.SemaphoreType.DMA(()),
-            pltpu.SemaphoreType.DMA(()),
+            pltpu.SemaphoreType.DMA((reps,)),
             pltpu.SemaphoreType.DMA((4,)),
             pltpu.SemaphoreType.DMA((2,)),
             pltpu.SemaphoreType.DMA((2,)),
@@ -314,32 +312,26 @@
         + 2
         * [
             pltpu.SemaphoreType.DMA(()),
-            pltpu.SemaphoreType.DMA((groups,)),
+            pltpu.SemaphoreType.DMA((GROUPS,)),
             pltpu.SemaphoreType.DMA((2,)),
             pltpu.SemaphoreType.DMA((2,)),
         ],
         compiler_params=pltpu.CompilerParams(
-            collective_id=0, has_side_effects=True, vmem_limit_bytes=63 << 20
+            collective_id=0, has_side_effects=True, vmem_limit_bytes=40 << 20
         ),
         name="shampoo_step",
     )(
-        gradient, block_lists.reshape(1, devices), block_counts.reshape(1, devices),
-        left_stats, right_stats,
+        keep(gradient), keep(block_lists.reshape(1, devices)), keep(block_counts.reshape(1, devices)),
+        keep(left_stats), keep(right_stats),
     )
     results = (direction, left_new, right_new)
     return pl.pallas_call(
         hand_over,
         out_shape=tuple(jax.ShapeDtypeStruct(x.shape, x.dtype) for x in results),
-        in_specs=[anywhere] * 3,
+        in_specs=[pl.BlockSpec(memory_space=pltpu.VMEM)] * 3,
         out_specs=(anywhere,) * 3,
-        scratch_shapes=[
-            pltpu.VMEM(left_stats.shape[1:], jnp.float32),
-            pltpu.VMEM(right_stats.shape[1:], jnp.float32),
-            pltpu.VMEM(direction.shape, jnp.bfloat16),
-            pltpu.SemaphoreType.DMA((3, PIECES)),
-            pltpu.SemaphoreType.DMA((3, PIECES)),
-        ],
-        compiler_params=pltpu.CompilerParams(vmem_limit_bytes=63 << 20),
+        scratch_shapes=[pltpu.SemaphoreType.DMA((3, PIECES))],
+        compiler_params=pltpu.CompilerParams(vmem_limit_bytes=16 << 20),
         name="hand_over",
     )(*results)
 

time: 60.6 us -> 57.9 us (0.955)
  Pallas kernels: 59.8 us -> 57.1 us
    pallas_call x1, Pallas kernels: 57.3 us -> 55.7 us  [local(): pl.pallas_call(functools.partial(kernel, reps, layers), out_shape=(pltpu....]
    pallas_call x1, Pallas kernels: 2.54 us -> 1.44 us  [local(): pl.pallas_call(hand_over, out_shape=tuple((jax.ShapeDtypeStruct(x.shape,...]
where the time goes in v3:
time: 57.9 us; the launch traced here: 57.7 us
  Pallas kernels  57.1 us (99%)
  between operations  0.64 us (1%)
    pallas_call x1, Pallas kernels, local(): pl.pallas_call(functools.partial(kernel, reps, layers), out_shape=(pltpu....  55.7 us
    pallas_call x1, Pallas kernels, local(): pl.pallas_call(hand_over, out_shape=tuple((jax.ShapeDtypeStruct(x.shape,...  1.44 us

profile of v3, /device:TPU:1, one launch (start us, length us, event | category | flops | bytes accessed | tf_op | source)
XLA Modules:
  0.0 57.7 jit_solution(10642060001987014312)
XLA Ops:
  0.6 55.7 %shampoo_step.1 = (bf16[64,4,512]{2,1,0:T(4,128)(2,1)S(1)}, f32[1,512,512]{2,1,0:T(8,128)S(1)}, f32[1,512,512]{2,1,0:T(8,128)S(1)}) custom-call(bf16[1,64,4,512]{3,2,1,0:T(4,128)(2,1)} %grad.1, s32[1,128]{1,0:T(1,128)} %bitcast.2, s32[1,128]{1,0:T(1,128)} %bitcast.3, f32[1,512,512]{2,1,0:T(8,128)} %left.1, f32[1,512,512]{2,1,0:T(8,128)} %right.1), custom_call_target="tpu_custom_call" | custom-call | tf_op jit(solution)/shard_map/shampoo_step/pallas_call | solution.py:272
  56.3 1.4 %hand_over.1 = (bf16[64,4,512]{2,1,0:T(4,128)(2,1)}, f32[1,512,512]{2,1,0:T(8,128)}, f32[1,512,512]{2,1,0:T(8,128)}) custom-call(bf16[64,4,512]{2,1,0:T(4,128)(2,1)S(1)} %get-tuple-element.6.direction, f32[1,512,512]{2,1,0:T(8,128)S(1)} %get-tuple-element.7.left, f32[1,512,512]{2,1,0:T(8,128)S(1)} %get-tuple-element.8.right), custom_call_target="tpu_custom_call" | custom-call | tf_op jit(solution)/shard_map/hand_over/pallas_call | solution.py:328

commit v4 on v3

--- a/solution.py
+++ b/solution.py
@@ -59,11 +59,11 @@
     pltpu.make_async_copy(ref, ref, sem).wait()
 
 
-def exchange(reps, layers, cuts, send, mid, out, a_send, a_recv, b_send, b_recv):
+def exchange(reps, layers, cuts, order_a, send, mid, out, a_send, a_recv, b_send, b_recv):
     rep, _, layer, lane = position()
     order = near_first(layers)
     groups = groups_of(layers, cuts)
-    for slot in range(1, layers) if cuts else range(layers - 1, 0, -1):
+    for slot in order_a:
         there = (layer - order[slot] + layers) % layers
         group = [lo <= slot < hi for lo, hi in groups].index(True)
         pltpu.make_async_remote_copy(
@@ -79,7 +79,7 @@
         if max(lo, 1) < hi:
             take(mid.at[:, max(lo, 1) : hi], a_recv.at[group])
         for turn in [t for t in (2, 1, 3) if t < reps] + [0]:
-            for hop in (4, 3, 5, 2, 6, 1, 7, 0):
+            for hop in (4, 6, 2, 5, 3, 7, 1, 0):
                 if turn or hop:
                     target = (lane + hop) % LANES
                     pltpu.make_async_remote_copy(
@@ -195,7 +195,8 @@
             send[z, l] = total[block]
 
     pl.semaphore_wait(relay, 2)
-    exchange(reps, layers, (), send, mid_in, blocks, a_send, a_recv, b_send, b_recv)
+    far_first = range(layers - 1, 0, -1)
+    exchange(reps, layers, (3,), far_first, send, mid_in, blocks, a_send, a_recv, b_send, b_recv)
 
     for part in range(reps):
         for slot_at, offset_at in enumerate(near_first(layers)):
@@ -225,7 +226,7 @@
     grafted = (own * (grad_norm / shaped_norm)).astype(jnp.bfloat16)
     piece[...] = grafted.reshape(piece.shape)
 
-    exchange(reps, layers, (7,), piece, mid_out, arrived, c_send, c_recv, d_send, d_recv)
+    exchange(reps, layers, (5, 11), range(1, layers), piece, mid_out, arrived, c_send, c_recv, d_send, d_recv)
     put_table.wait()
 
     @pl.loop(0, block_total // 8)

time: 57.9 us -> 57.1 us (0.986)
  Pallas kernels: 57.1 us -> 56.3 us
    pallas_call x1, Pallas kernels: 55.7 us -> 54.8 us  [local(): pl.pallas_call(functools.partial(kernel, reps, layers), out_shape=(pltpu....]
where the time goes in v4:
time: 57.1 us; the launch traced here: 56.9 us
  Pallas kernels  56.3 us (99%)
  between operations  0.64 us (1%)
    pallas_call x1, Pallas kernels, local(): pl.pallas_call(functools.partial(kernel, reps, layers), out_shape=(pltpu....  54.8 us
    pallas_call x1, Pallas kernels, local(): pl.pallas_call(hand_over, out_shape=tuple((jax.ShapeDtypeStruct(x.shape,...  1.44 us

profile of v4, /device:TPU:1, one launch (start us, length us, event | category | flops | bytes accessed | tf_op | source)
XLA Modules:
  0.0 56.9 jit_solution(7390734738173001390)
XLA Ops:
  0.6 54.8 %shampoo_step.1 = (bf16[64,4,512]{2,1,0:T(4,128)(2,1)S(1)}, f32[1,512,512]{2,1,0:T(8,128)S(1)}, f32[1,512,512]{2,1,0:T(8,128)S(1)}) custom-call(bf16[1,64,4,512]{3,2,1,0:T(4,128)(2,1)} %grad.1, s32[1,128]{1,0:T(1,128)} %bitcast.2, s32[1,128]{1,0:T(1,128)} %bitcast.3, f32[1,512,512]{2,1,0:T(8,128)} %left.1, f32[1,512,512]{2,1,0:T(8,128)} %right.1), custom_call_target="tpu_custom_call" | custom-call | tf_op jit(solution)/shard_map/shampoo_step/pallas_call | solution.py:273
  55.5 1.4 %hand_over.1 = (bf16[64,4,512]{2,1,0:T(4,128)(2,1)}, f32[1,512,512]{2,1,0:T(8,128)}, f32[1,512,512]{2,1,0:T(8,128)}) custom-call(bf16[64,4,512]{2,1,0:T(4,128)(2,1)S(1)} %get-tuple-element.6.direction, f32[1,512,512]{2,1,0:T(8,128)S(1)} %get-tuple-element.7.left, f32[1,512,512]{2,1,0:T(8,128)S(1)} %get-tuple-element.8.right), custom_call_target="tpu_custom_call" | custom-call | tf_op jit(solution)/shard_map/hand_over/pallas_call | solution.py:329

commit v5 on v4

--- a/solution.py
+++ b/solution.py
@@ -125,10 +125,10 @@
 
 def kernel(
     reps, layers, grad, ids_in, counts_in, left, right,
-    direction, left_out, right_out,
+    arrived, table, left_out, right_out,
     local, parts, total, send, mid_in, blocks, g_ref, stat_left, stat_right, left_new, right_new, shaped,
-    piece, mid_out, arrived, table, table_smem, ids, counts, ids_row, counts_row,
-    relay, r_send, r_recv, fetch_sems, small_sems, stat_sems, put_sems, table_sem,
+    piece, mid_out, ids, counts, ids_row, counts_row,
+    relay, r_send, r_recv, fetch_sems, small_sems, stat_sems, put_sems,
     a_send, a_recv, b_send, b_recv, c_send, c_recv, d_send, d_recv,
 ):
     rep, place, layer, lane = position()
@@ -179,8 +179,6 @@
     slot = jnp.where(offset <= layers // 2, jnp.maximum(2 * offset - 1, 0), 2 * (layers - offset))
     spot = slot * LANES + worker % LANES
     table[...] = jnp.max(jnp.where(match, spot, 0), axis=0, keepdims=True)
-    put_table = pltpu.make_async_copy(table, table_smem, table_sem)
-    put_table.start()
 
     take(parts.at[1:reps], r_recv)
     acc = local[rep].astype(jnp.float32)
@@ -227,36 +225,42 @@
     piece[...] = grafted.reshape(piece.shape)
 
     exchange(reps, layers, (5, 11), range(1, layers), piece, mid_out, arrived, c_send, c_recv, d_send, d_recv)
-    put_table.wait()
-
-    @pl.loop(0, block_total // 8)
-    def _(group):
-        for k in range(8):
-            block = group * 8 + k
-            spot_at = table_smem[0, block]
-            for part in range(reps):
-                direction[block, :, part * width : (part + 1) * width] = arrived[
-                    part, spot_at // LANES, spot_at % LANES
-                ]
-
     take(parts.at[1:reps], r_send)
     exchange_end(reps, layers, mid_in, blocks, a_send, b_send)
     exchange_end(reps, layers, mid_out, arrived, c_send, d_send)
 
 
-def hand_over(direction, left, right, direction_out, left_out, right_out, sems):
+def hand_over(
+    arrived, table, left, right, direction_out, left_out, right_out, direction, spots, sems, own_sems
+):
+    reps, _, _, _, width = arrived.shape
+    get_table = pltpu.make_async_copy(table, spots, own_sems.at[0])
+    get_table.start()
     copies = []
-    for k, (src, dst) in enumerate(
-        [(left.at[0], left_out.at[0]), (right.at[0], right_out.at[0]), (direction, direction_out)]
-    ):
+    for k, (src, dst) in enumerate([(left.at[0], left_out.at[0]), (right.at[0], right_out.at[0])]):
         step = src.shape[0] // PIECES
         for p in range(PIECES):
             span = pl.ds(p * step, step)
             copies.append(pltpu.make_async_copy(src.at[span], dst.at[span], sems.at[k, p]))
     for copy in copies:
         copy.start()
+    get_table.wait()
+
+    @pl.loop(0, direction.shape[0] // 8)
+    def _(group):
+        for k in range(8):
+            block = group * 8 + k
+            spot = spots[0, block]
+            for part in range(reps):
+                direction[block, :, part * width : (part + 1) * width] = arrived[
+                    part, spot // LANES, spot % LANES
+                ]
+
+    put = pltpu.make_async_copy(direction, direction_out, own_sems.at[1])
+    put.start()
     for copy in copies:
         copy.wait()
+    put.wait()
 
 
 def local(gradient, left_stats, right_stats, block_lists, block_counts):
@@ -270,15 +274,16 @@
     def keep(x):
         return pltpu.with_memory_space_constraint(x, pltpu.HBM)
 
-    direction, left_new, right_new = pl.pallas_call(
+    arrived, table, left_new, right_new = pl.pallas_call(
         functools.partial(kernel, reps, layers),
         out_shape=(
-            pltpu.VMEM((block_total, dev_rows, cols), jnp.bfloat16),
+            pltpu.VMEM((reps, layers, LANES, dev_rows, width), jnp.bfloat16),
+            pltpu.VMEM((1, devices), jnp.int32),
             pltpu.VMEM(left_stats.shape, jnp.float32),
             pltpu.VMEM(right_stats.shape, jnp.float32),
         ),
         in_specs=[anywhere] * 5,
-        out_specs=(vmem, vmem, vmem),
+        out_specs=(vmem, vmem, vmem, vmem),
         scratch_shapes=[
             pltpu.VMEM((reps, block_total, dev_rows, width), jnp.bfloat16),
             pltpu.VMEM((reps, block_total, dev_rows, width), jnp.bfloat16),
@@ -294,9 +299,6 @@
             pltpu.VMEM((rows, cols), jnp.float32),
             pltpu.VMEM((layers, LANES, dev_rows, width), jnp.bfloat16),
             pltpu.VMEM((LANES, layers, dev_rows, width), jnp.bfloat16),
-            pltpu.VMEM((reps, layers, LANES, dev_rows, width), jnp.bfloat16),
-            pltpu.VMEM((1, devices), jnp.int32),
-            pltpu.SMEM((1, devices), jnp.int32),
             pltpu.SMEM((1, devices), jnp.int32),
             pltpu.SMEM((1, devices), jnp.int32),
             pltpu.VMEM((1, devices), jnp.int32),
@@ -308,7 +310,6 @@
             pltpu.SemaphoreType.DMA((4,)),
             pltpu.SemaphoreType.DMA((2,)),
             pltpu.SemaphoreType.DMA((2,)),
-            pltpu.SemaphoreType.DMA(()),
         ]
         + 2
         * [
@@ -325,16 +326,23 @@
         keep(gradient), keep(block_lists.reshape(1, devices)), keep(block_counts.reshape(1, devices)),
         keep(left_stats), keep(right_stats),
     )
-    results = (direction, left_new, right_new)
+    results = (
+        jax.ShapeDtypeStruct((block_total, dev_rows, cols), jnp.bfloat16), left_new, right_new
+    )
     return pl.pallas_call(
         hand_over,
         out_shape=tuple(jax.ShapeDtypeStruct(x.shape, x.dtype) for x in results),
-        in_specs=[pl.BlockSpec(memory_space=pltpu.VMEM)] * 3,
+        in_specs=[vmem] * 4,
         out_specs=(anywhere,) * 3,
-        scratch_shapes=[pltpu.SemaphoreType.DMA((3, PIECES))],
+        scratch_shapes=[
+            pltpu.VMEM((block_total, dev_rows, cols), jnp.bfloat16),
+            pltpu.SMEM((1, devices), jnp.int32),
+            pltpu.SemaphoreType.DMA((2, PIECES)),
+            pltpu.SemaphoreType.DMA((2,)),
+        ],
         compiler_params=pltpu.CompilerParams(vmem_limit_bytes=16 << 20),
         name="hand_over",
-    )(*results)
+    )(arrived, table, left_new, right_new)
 
 
 def solution(mesh):

time: 57.1 us -> 57.3 us (level)
  no operation moved by 1% of the time
where the time goes in v5:
time: 57.3 us; the launch traced here: 57.1 us
  Pallas kernels  56.5 us (99%)
  between operations  0.64 us (1%)
    pallas_call x1, Pallas kernels, local(): pl.pallas_call(functools.partial(kernel, reps, layers), out_shape=(pltpu....  54.7 us
    pallas_call x1, Pallas kernels, local(): pl.pallas_call(hand_over, out_shape=tuple((jax.ShapeDtypeStruct(x.shape,...  1.78 us

profile of v5, /device:TPU:1, one launch (start us, length us, event | category | flops | bytes accessed | tf_op | source)
XLA Modules:
  0.0 57.1 jit_solution(5140974662974290360)
XLA Ops:
  0.6 54.7 %shampoo_step.1 = (bf16[4,16,8,4,128]{4,3,2,1,0:T(4,128)(2,1)S(1)}, s32[1,128]{1,0:T(1,128)S(1)}, f32[1,512,512]{2,1,0:T(8,128)S(1)}, f32[1,512,512]{2,1,0:T(8,128)S(1)}) custom-call(bf16[1,64,4,512]{3,2,1,0:T(4,128)(2,1)} %grad.1, s32[1,128]{1,0:T(1,128)} %bitcast.2, s32[1,128]{1,0:T(1,128)} %bitcast.3, f32[1,512,512]{2,1,0:T(8,128)} %left.1, ...), custom_call_target="tpu_custom_call" | custom-call | tf_op jit(solution)/shard_map/shampoo_step/pallas_call | solution.py:277
  55.4 1.8 %hand_over.1 = (bf16[64,4,512]{2,1,0:T(4,128)(2,1)}, f32[1,512,512]{2,1,0:T(8,128)}, f32[1,512,512]{2,1,0:T(8,128)}) custom-call(bf16[4,16,8,4,128]{4,3,2,1,0:T(4,128)(2,1)S(1)} %get-tuple-element.7.arrived, s32[1,128]{1,0:T(1,128)S(1)} %get-tuple-element.8.table, f32[1,512,512]{2,1,0:T(8,128)S(1)} %get-tuple-element.9.left, ...), custom_call_target="tpu_custom_call" | custom-call | tf_op jit(solution)/shard_map/hand_over/pallas_call | solution.py:332
